TPU v7x, 256 devices: a whole 4x4x8 slice. The times are simulated.
256 devices in a mesh: items: 32 (over x, y, core), codes: 8 (over z).
Axes of the slice: x: 4, y: 4, z: 8, core: 2. Of those that a mesh axis runs over, the one named last changes fastest.
Arguments:
- residuals: bfloat16 [65536, 256], P('items', 'codes'), may hold values from -6 to 6
- codebook: bfloat16 [8192, 256], P('codes'), may hold values from -6 to 6
Outputs:
- soft_codes: float32 [65536, 256], P('items', 'codes')
- items_scale: float32 [65536], P('items')
- code_weights: float32 [8192], P('codes')
All inputs are finite; a program needn't handle non-finite values.
Results may differ from a plain program's by a relative error of at most 0.0014.
Values may be sent and summed in bfloat16 or wider, within the bound.
A program may use at most 64 MiB of HBM per device.

v0:
```python
import jax
import jax.numpy as jnp
from jax import lax
from jax.sharding import PartitionSpec as P

F = 256
ITERS = 3


eps_value = 1e-06
entropic_smoothing = 32.0
affinity_shift = 2.0


def inverse_scale(values):
    wide = values.astype(jnp.float32)
    return lax.rsqrt(jnp.mean(wide * wide, axis=-1) + eps_value)


def kernel_tile(rows, row_inv, codes, reciprocal_centroid_factor):
    dots = jnp.dot(rows, codes.T, preferred_element_type=jnp.float32)
    angular_affinity = dots * row_inv[:, None] * reciprocal_centroid_factor[None, :] / F
    return jnp.exp(entropic_smoothing * angular_affinity - affinity_shift)


def mixture_block(rows, scales, codes, reciprocal_centroid_factor, weights, codebook_entry_count):
    tile = kernel_tile(rows, scales, codes, reciprocal_centroid_factor)
    assignment_shares = (tile * (weights / codebook_entry_count)[None, :]).astype(jnp.bfloat16)
    return jnp.dot(assignment_shares, codes, preferred_element_type=jnp.float32)


def shards(residuals, codebook):
    gathered = lax.all_gather(residuals, "codes", axis=1, tiled=True)
    row_count = gathered.shape[0]
    block = min(512, row_count)
    count = row_count // block
    row_blocks = gathered.reshape(count, block, F)
    row_scales = inverse_scale(gathered).reshape(count, block)
    reciprocal_centroid_factor = inverse_scale(codebook)
    local_codes = codebook.shape[0]
    residual_item_count = row_count * lax.axis_size("items")
    codebook_entry_count = local_codes * lax.axis_size("codes")

    def refresh_right_factors(items_scale):

        def column_step(total, item):
            rows, scales, weights = item
            tile = kernel_tile(rows, scales, codebook, reciprocal_centroid_factor)
            return (total + jnp.sum(tile * weights[:, None], axis=0), None)

        totals, discarded_output = lax.scan(
            column_step,
            jnp.zeros((local_codes,), jnp.float32),
            (row_blocks, row_scales, items_scale.reshape(count, block)),
        )
        return residual_item_count / lax.psum(totals, "items")

    def update_rows(code_weights):

        def left_factor_update(item):
            rows, scales = item
            tile = kernel_tile(rows, scales, codebook, reciprocal_centroid_factor)
            return jnp.sum(tile * code_weights[None, :], axis=1)

        sums = lax.map(left_factor_update, (row_blocks, row_scales)).reshape(row_count)
        return codebook_entry_count / lax.psum(sums, "codes")

    items_scale = jnp.ones((row_count,), jnp.float32)
    for iteration in range(ITERS - 1):
        code_weights = refresh_right_factors(items_scale)
        items_scale = update_rows(code_weights)
    code_weights = refresh_right_factors(items_scale)
    items_scale = update_rows(code_weights)

    def soft_step(item):
        rows, scales = item
        return mixture_block(
            rows, scales, codebook, reciprocal_centroid_factor, code_weights, codebook_entry_count
        )

    parts = lax.map(soft_step, (row_blocks, row_scales)).reshape(row_count, F)
    mixture = lax.psum_scatter(parts, "codes", scatter_dimension=1, tiled=True)
    soft_codes = items_scale[:, None] * mixture
    return (soft_codes, items_scale, code_weights)


def solution(mesh):
    placed = (P("items", "codes"), P("codes", None))
    return jax.shard_map(
        shards,
        mesh=mesh,
        in_specs=placed,
        out_specs=(P("items", "codes"), P("items"), P("codes")),
        check_vma=False,
    )
```

profile of v0, /device:TPU:2, one launch (start us, length us, event | category | flops | bytes accessed | tf_op | source)
XLA Modules:
  0.0 367.7 jit_solution(2010930158032384924)
XLA Ops:
  8.0 1.3 multiply_reduce_fusion.6
  9.3 42.2 %all-gather.2.cloned.1.call-done = bf16[2048,256]{0,1:T(8,128)(2,1)} async-done(((bf16[2048,32]{0,1:T(8,128)(2,1)}), bf16[2048,256]{0,1:T(8,128)(2,1)}) %all-gather.2.cloned.1.call-update) | async-done | bytes 1048592 | tf_op jit(solution)/shard_map/all_gather | solution.py:33
  51.5 1.5 multiply_reduce_fusion.5
  53.0 1.5 copy.5
  54.5 7.2 %while.91 = (s32[]{:T(128)}, f32[1024]{0:T(1024)S(1)}, bf16[4,512,256]{2,1,0:T(8,128)(2,1)S(1)}, bf16[1024,256]{1,0:T(8,128)(2,1)}, f32[4,512]{1,0:T(4,128)S(1)}, /*index=5*/f32[1024]{0:T(1024)S(1)}, s32[]{:T(128)}, s32[]{:T(128)}) while((s32[]{:T(128)}, f32[1024]{0:T(1024)S(1)}, bf16[4,512,256]{2,1,0:T(8,128)(2,1)S(1)}, ...), condition=%wide.region_4.5_spmd.clone, body=%wide.region_2.4_spmd.clone.sunk | while | flops 271057920 | bytes 813159 | solution.py:51
  54.5 1.7 exponential_reduce_fusion.2
  56.3 1.8 exponential_reduce_fusion.2
  58.1 1.7 exponential_reduce_fusion.2
  59.9 1.8 exponential_reduce_fusion.2
  61.7 53.0 %psum.42 = f32[1024]{0:T(1024)S(1)} all-reduce(f32[1024]{0:T(1024)S(1)} %get-tuple-element.621), channel_id=1, replica_groups=mesh['items'=32,'codes'=8] {'items'}, use_global_device_ids=true, to_apply=%region_5.6 | all-reduce | flops 1024 | bytes 8192 | tf_op jit(solution)/shard_map/psum | solution.py:56
  114.7 7.8 %while.87 = (s32[]{:T(128)}, f32[4,512]{1,0:T(4,128)S(1)}, bf16[4,512,256]{2,1,0:T(8,128)(2,1)S(1)}, bf16[1024,256]{1,0:T(8,128)(2,1)}, f32[4,512]{1,0:T(4,128)S...) while((s32[]{:T(128)}, f32[4,512]{1,0:T(4,128)S(1)}, ...), condition=%wide.region_8.9_spmd, body=%wide.region_6.8_spmd.sunk | while | flops 271580672 | bytes 807017 | solution.py:65
  114.7 1.9 multiply_reduce_fusion.12
  116.7 1.9 multiply_reduce_fusion.12
  118.6 1.9 multiply_reduce_fusion.12
  120.6 1.9 multiply_reduce_fusion.12
  122.5 16.1 %psum.43 = f32[2048]{0:T(1024)S(1)} all-reduce(f32[2048]{0:T(1024)S(1)} %bitcast.127), channel_id=1, replica_groups=mesh['items'=32,'codes'=8] {'codes'}, use_global_device_ids=true, to_apply=%region_9.10 | all-reduce | flops 2048 | bytes 16384 | tf_op jit(solution)/shard_map/psum | solution.py:66
  138.6 7.5 %while.92 = (s32[]{:T(128)}, f32[1024]{0:T(1024)S(1)}, bf16[4,512,256]{2,1,0:T(8,128)(2,1)S(1)}, bf16[1024,256]{1,0:T(8,128)(2,1)}, f32[4,512]{1,0:T(4,128)S(1)}...) while((s32[]{:T(128)}, f32[1024]{0:T(1024)S(1)}, ...), condition=%wide.region_12.13_spmd.clone, body=%wide.region_10.12_spmd.clone.sunk | while | flops 271582208 | bytes 819311 | solution.py:51
  138.7 1.8 multiply_reduce_fusion.15
  140.5 1.8 multiply_reduce_fusion.15
  142.4 1.8 multiply_reduce_fusion.15
  144.3 1.8 multiply_reduce_fusion.15
  146.1 54.6 %psum.44 = f32[1024]{0:T(1024)S(1)} all-reduce(f32[1024]{0:T(1024)S(1)} %get-tuple-element.623), channel_id=1, replica_groups=mesh['items'=32,'codes'=8] {'items'}, use_global_device_ids=true, to_apply=%region_13.14 | all-reduce | flops 1024 | bytes 8192 | tf_op jit(solution)/shard_map/psum | solution.py:56
  200.8 7.8 %while.88 = (s32[]{:T(128)}, f32[4,512]{1,0:T(4,128)S(1)}, bf16[4,512,256]{2,1,0:T(8,128)(2,1)S(1)}, bf16[1024,256]{1,0:T(8,128)(2,1)}, f32[4,512]{1,0:T(4,128)S...) while((s32[]{:T(128)}, f32[4,512]{1,0:T(4,128)S(1)}, ...), condition=%wide.region_16.17_spmd, body=%wide.region_14.16_spmd.sunk | while | flops 271580672 | bytes 807017 | solution.py:65
  200.8 1.9 multiply_reduce_fusion.13
  202.8 1.9 multiply_reduce_fusion.13
  204.7 1.9 multiply_reduce_fusion.13
  206.7 1.9 multiply_reduce_fusion.13
  208.6 14.8 %psum.45 = f32[2048]{0:T(1024)S(1)} all-reduce(f32[2048]{0:T(1024)S(1)} %bitcast.128), channel_id=1, replica_groups=mesh['items'=32,'codes'=8] {'codes'}, use_global_device_ids=true, to_apply=%region_17.18 | all-reduce | flops 2048 | bytes 16384 | tf_op jit(solution)/shard_map/psum | solution.py:66
  223.4 7.5 %while.93 = (s32[]{:T(128)}, f32[1024]{0:T(1024)S(1)}, bf16[4,512,256]{2,1,0:T(8,128)(2,1)S(1)}, bf16[1024,256]{1,0:T(8,128)(2,1)}, f32[4,512]{1,0:T(4,128)S(1)}...) while((s32[]{:T(128)}, f32[1024]{0:T(1024)S(1)}, ...), condition=%wide.region_20.21_spmd.clone, body=%wide.region_18.20_spmd.clone.sunk | while | flops 271582208 | bytes 819311 | solution.py:51
  223.5 1.8 multiply_reduce_fusion.16
  225.3 1.8 multiply_reduce_fusion.16
  227.2 1.8 multiply_reduce_fusion.16
  229.1 1.8 multiply_reduce_fusion.16
  230.9 62.7 %psum.46 = f32[1024]{0:T(1024)S(1)} all-reduce(f32[1024]{0:T(1024)S(1)} %get-tuple-element.625), channel_id=1, replica_groups=mesh['items'=32,'codes'=8] {'items'}, use_global_device_ids=true, to_apply=%region_21.22 | all-reduce | flops 1024 | bytes 8192 | tf_op jit(solution)/shard_map/psum | solution.py:56
  293.6 8.9 %while.90 = (s32[]{:T(128)}, f32[4,512,256]{2,1,0:T(8,128)S(1)}, bf16[4,512,256]{2,1,0:T(8,128)(2,1)S(1)}, bf16[1024,256]{1,0:T(8,128)(2,1)}, f32[4,512]{1,0:T(4...) while((s32[]{:T(128)}, f32[4,512,256]{2,1,0:T(8,128)S(1)}, ...), condition=%wide.region_27.28_spmd, body=%wide.region_26.27_spmd.sunk | while | flops 540017664 | bytes 1858649 | solution.py:81
  293.6 2.2 fusion.67
  295.9 2.2 fusion.67
  298.1 2.2 fusion.67
  300.3 2.2 fusion.67
  302.5 1.9 copy.7
  304.4 1.0 copy-done
  305.4 3.6 while.89
  306.3 0.8 multiply_reduce_fusion.14
  307.2 0.8 multiply_reduce_fusion.14
  308.1 0.8 multiply_reduce_fusion.14
  309.1 16.3 %psum.47 = f32[2048]{0:T(1024)S(1)} all-reduce(f32[2048]{0:T(1024)S(1)} %bitcast.129), channel_id=1, replica_groups=mesh['items'=32,'codes'=8] {'codes'}, use_global_device_ids=true, to_apply=%region_25.26 | all-reduce | flops 2048 | bytes 16384 | tf_op jit(solution)/shard_map/psum | solution.py:66
  325.4 33.8 %reduce-scatter.2.cloned.1.call-done = f32[2048,32]{0,1:T(8,128)} async-done(((f32[2048,256]{0,1:T(8,128)}), f32[2048,32]{0,1:T(8,128)}) %reduce-scatter.2.cloned.1.call-update) | async-done | bytes 262160 | tf_op jit(solution)/shard_map/reduce_scatter | solution.py:82
  359.1 1.7 broadcast_multiply_fusion.1
  (87 shorter events, 2.6 us)
Async XLA Ops:
  7.2 44.3 %all-gather.2.cloned.1.call-start = ((), (), s32[]{:S(2)}) async-start(), calls=%async_computation.1 | async-start | bytes 1179648 | tf_op jit(solution)/shard_map/all_gather | solution.py:33
  7.9 351.2 %reduce-scatter.2.cloned.1.call-start = ((), (), s32[]{:S(2)}) async-start(), calls=%async_computation.2 | async-start | bytes 2359296 | tf_op jit(solution)/shard_map/reduce_scatter | solution.py:82
  304.4 1.0 copy-start
  309.0 51.8 %copy-start.1 = (f32[1024]{0:T(1024)}, f32[1024]{0:T(1024)S(1)}, u32[]{:S(2)}) copy-start(f32[1024]{0:T(1024)S(1)} %get-tuple-element.1308) | copy-start | bytes 12292
  325.3 35.5 %copy-start.2 = (f32[2048]{0:T(1024)}, f32[2048]{0:T(1024)S(1)}, u32[]{:S(2)}) copy-start(f32[2048]{0:T(1024)S(1)} %broadcast_divide_fusion) | copy-start | bytes 24580
Sparse Core Ops, SparseCore 0:
  9.8 41.6 all-gather.1
  304.5 54.5 reduce-scatter.1
where the time goes:
time: 369 us; the launch traced here: 368 us
  blocking collectives  217 us (59%)
  waiting for transfers between devices  76.7 us (21%)
  matrix products  48.5 us (13%)
  between operations  14.3 us (4%)
  local copies, waits for them, and re-layouts  5.22 us (1%)
  other arithmetic  4.53 us (1%)
    psum x3, blocking collectives, refresh_right_factors(): return residual_item_count / lax.psum(totals, 'items')  170 us
    psum x3, blocking collectives, update_rows(): return codebook_entry_count / lax.psum(sums, 'codes')  47.1 us
    all_gather x1, waiting for transfers between devices, shards(): gathered = lax.all_gather(residuals, 'codes', axis=1, tiled=True)  42.2 us
    dot_general x24, matrix products, kernel_tile(): dots = jnp.dot(rows, codes.T, preferred_element_type=jnp.float32)  39.8 us
    reduce_scatter x1, waiting for transfers between devices, shards(): mixture = lax.psum_scatter(parts, 'codes', scatter_dimension=1, tiled=True)  33.8 us
    dot_general x4, matrix products, mixture_block(): return jnp.dot(assignment_shares, codes, preferred_element_type=jnp.float32)  8.71 us
  transfers between devices with their start and end apart: 2, of which 2 were waited for; matrix products, arithmetic and copies ran while one was open for 1% of the time, Pallas kernels for 0%

commit v1 on v0

v1 whole, which is shorter than its diff:
```python
import functools

import jax
import jax.numpy as jnp
from jax import lax
from jax.experimental import pallas as pl
from jax.experimental.pallas import tpu as pltpu
from jax.sharding import PartitionSpec as P

F = 256
ITERS = 3
EPS = 1e-06
SMOOTHING = 32.0
SHIFT = 2.0
LOG2E = 1.4426950408889634

LANES = 128
CHUNK = 512
TILE = 128
MESH = pl.DeviceIdType.MESH


def kernel(
    items_n, codes_n, total_items, total_codes,
    rt_hbm, cb_hbm, parts_ref, s_ref, w_ref,
    cb, R, K, inv_row, inv_col, tacc, W, tsend, colbuf, rowbuf,
    in_sem, ring_send, ring_recv, col_send, col_recv, row_send, row_recv,
):
    me_i = lax.axis_index("items")
    me_z = lax.axis_index("codes")
    rows = rt_hbm.shape[1]
    codes = cb_hbm.shape[0]
    feats = rt_hbm.shape[0]
    chunks = rows // CHUNK
    right = lax.rem(me_z + 1, codes_n)
    left = lax.rem(me_z + codes_n - 1, codes_n)
    half = codes_n // 2

    def block(c, z):
        return R.at[c, pl.ds(pl.multiple_of(z * feats, feats), feats), :]

    own = [
        pltpu.make_async_copy(
            rt_hbm.at[:, c * CHUNK:(c + 1) * CHUNK], block(c, me_z), in_sem.at[c]
        )
        for c in range(chunks)
    ]
    for copy in own:
        copy.start()
    load_cb = pltpu.make_async_copy(cb_hbm, cb, in_sem.at[chunks])
    load_cb.start()

    barrier = pltpu.get_barrier_semaphore()

    def greet_items(k, carry):
        pl.semaphore_signal(
            barrier, inc=1, device_id={"items": lax.rem(me_i + k, items_n)}, device_id_type=MESH
        )
        return carry

    def greet_codes(k, carry):
        pl.semaphore_signal(
            barrier, inc=1, device_id={"codes": lax.rem(me_z + k, codes_n)}, device_id_type=MESH
        )
        return carry

    lax.fori_loop(1, codes_n, greet_codes, 0)
    lax.fori_loop(1, items_n, greet_items, 0)
    pl.semaphore_wait(barrier, items_n + codes_n - 2)

    def hop(direction, h, c):
        z = me_z - (h - 1) if direction == 0 else me_z + (h - 1)
        z = lax.rem(z + codes_n, codes_n)
        ref = block(c, z)
        return pltpu.make_async_remote_copy(
            src_ref=ref, dst_ref=ref,
            send_sem=ring_send.at[direction, h - 1, c],
            recv_sem=ring_recv.at[direction, h - 1, c],
            device_id={"codes": right if direction == 0 else left},
            device_id_type=MESH,
        )

    def goes(direction, h, c):
        return h < half or (h == half and (c < chunks // 2) == (direction == 0))

    for c in range(chunks):
        own[c].wait()
        for d in range(2):
            if goes(d, 1, c):
                hop(d, 1, c).start()
    load_cb.wait()

    wide = cb[...].astype(jnp.float32)
    inv_col[...] = jnp.broadcast_to(
        lax.rsqrt(jnp.mean(wide * wide, axis=1, keepdims=True) + EPS), inv_col.shape
    )
    tacc[...] = jnp.zeros_like(tacc)

    for h in range(1, half + 1):
        for c in range(chunks):
            for d in range(2):
                if goes(d, h, c):
                    hop(d, h, c).wait_recv()
                    if goes(d, h + 1, c):
                        hop(d, h + 1, c).start()

    for c in range(chunks):
        r_wide = R[c].astype(jnp.float32)
        inv_row[...] = lax.rsqrt(
            jnp.mean(r_wide * r_wide, axis=0, keepdims=True) + EPS
        ) * (SMOOTHING * LOG2E / F)

        def tile_step(m, carry, c=c):
            at = pl.ds(pl.multiple_of(m * TILE, TILE), TILE)
            dots = jnp.dot(cb[at, :], R[c], preferred_element_type=jnp.float32)
            scale = inv_col[at, :]
            total = tacc[at, :]
            for q in range(CHUNK // LANES):
                lanes = slice(q * LANES, (q + 1) * LANES)
                value = jnp.exp2(dots[:, lanes] * inv_row[:, lanes] * scale - SHIFT * LOG2E)
                K[at, c * CHUNK + q * LANES:c * CHUNK + (q + 1) * LANES] = value
                total = total + value
            tacc[at, :] = total
            return carry

        lax.fori_loop(0, codes // TILE, tile_step, 0)

    groups = codes // 8
    lane_chunks = rows // LANES

    def exchange(buf, it, mine, count, axis, send_sem, recv_sem):
        def send(k, carry):
            pltpu.make_async_remote_copy(
                src_ref=buf.at[it, mine], dst_ref=buf.at[it, mine],
                send_sem=send_sem.at[it], recv_sem=recv_sem.at[it],
                device_id={axis: lax.rem(mine + k, count)}, device_id_type=MESH,
            ).start()
            return carry

        lax.fori_loop(1, count, send, 0)

    def all_but_one(buf, it, count, sem):
        ref = buf.at[it, pl.ds(0, count - 1)]
        return pltpu.make_async_copy(ref, ref, sem.at[it])

    for it in range(ITERS):
        if it > 0:
            s_bcast = [
                jnp.broadcast_to(s_ref[q:q + 1, :], (8, LANES)) for q in range(lane_chunks)
            ]

            def col_step(g, carry):
                at = pl.ds(pl.multiple_of(g * 8, 8), 8)
                total = K[at, 0:LANES] * s_bcast[0]
                for q in range(1, lane_chunks):
                    total = total + K[at, q * LANES:(q + 1) * LANES] * s_bcast[q]
                tacc[at, :] = total
                return carry

            lax.fori_loop(0, groups, col_step, 0, unroll=4)
        for b in range(codes // LANES):
            blockT = jnp.transpose(tacc[b * LANES:(b + 1) * LANES, :])
            tsend[b:b + 1, :] = jnp.sum(blockT, axis=0, keepdims=True)
        colbuf[it, me_i] = tsend[...]
        exchange(colbuf, it, me_i, items_n, "items", col_send, col_recv)
        all_but_one(colbuf, it, items_n, col_recv).wait()
        w = total_items / jnp.sum(colbuf[it], axis=0)
        w_ref[...] = w
        for b in range(codes // LANES):
            W[b * LANES:(b + 1) * LANES, :] = jnp.transpose(
                jnp.broadcast_to(w[b:b + 1, :], (LANES, LANES))
            )

        def row_step(g, acc):
            at = pl.ds(pl.multiple_of(g * 8, 8), 8)
            weight = W[at, :]
            return tuple(
                acc[q] + K[at, q * LANES:(q + 1) * LANES] * weight for q in range(lane_chunks)
            )

        acc = lax.fori_loop(
            0, groups, row_step,
            tuple(jnp.zeros((8, LANES), jnp.float32) for _ in range(lane_chunks)), unroll=4,
        )
        for q in range(lane_chunks):
            s_ref[q:q + 1, :] = jnp.sum(acc[q], axis=0, keepdims=True)
        rowbuf[it, me_z] = s_ref[...]
        exchange(rowbuf, it, me_z, codes_n, "codes", row_send, row_recv)
        if it == ITERS - 1:
            def soft_step(n, carry):
                lanes = pl.ds(pl.multiple_of(n * 256, 256), 256)
                weight = W[...] * (1.0 / total_codes)
                shares = (K[:, lanes] * jnp.concatenate([weight, weight], axis=1)).astype(jnp.bfloat16)
                parts_ref[:, lanes] = lax.dot_general(
                    cb[...], shares, (((0,), (0,)), ((), ())), preferred_element_type=jnp.float32
                )
                return carry

            lax.fori_loop(0, rows // 256, soft_step, 0)
        all_but_one(rowbuf, it, codes_n, row_recv).wait()
        s_ref[...] = total_codes / jnp.sum(rowbuf[it], axis=0)

    for it in range(ITERS):
        all_but_one(colbuf, it, items_n, col_send).wait()
        all_but_one(rowbuf, it, codes_n, row_send).wait()
    for h in range(1, half + 1):
        for c in range(chunks):
            for d in range(2):
                if goes(d, h, c):
                    hop(d, h, c).wait_send()


def shards(residuals, codebook):
    items_n, codes_n = lax.axis_size("items"), lax.axis_size("codes")
    rows, feats = residuals.shape
    codes = codebook.shape[0]
    chunks = rows // CHUNK
    half = codes_n // 2
    f32 = jnp.float32
    any_space = pl.BlockSpec(memory_space=pl.ANY)
    vmem = pl.BlockSpec(memory_space=pltpu.VMEM)
    parts, items_scale, code_weights = pl.pallas_call(
        functools.partial(
            kernel, items_n, codes_n, float(rows * items_n), float(codes * codes_n)
        ),
        out_shape=(
            jax.ShapeDtypeStruct((F, rows), f32),
            jax.ShapeDtypeStruct((rows // LANES, LANES), f32),
            jax.ShapeDtypeStruct((codes // LANES, LANES), f32),
        ),
        in_specs=[any_space, any_space],
        out_specs=(vmem, vmem, vmem),
        scratch_shapes=[
            pltpu.VMEM((codes, F), jnp.bfloat16),
            pltpu.VMEM((chunks, F, CHUNK), jnp.bfloat16),
            pltpu.VMEM((codes, rows), f32),
            pltpu.VMEM((1, CHUNK), f32),
            pltpu.VMEM((codes, LANES), f32),
            pltpu.VMEM((codes, LANES), f32),
            pltpu.VMEM((codes, LANES), f32),
            pltpu.VMEM((codes // LANES, LANES), f32),
            pltpu.VMEM((ITERS, items_n, codes // LANES, LANES), f32),
            pltpu.VMEM((ITERS, codes_n, rows // LANES, LANES), f32),
            pltpu.SemaphoreType.DMA((chunks + 1,)),
            pltpu.SemaphoreType.DMA((2, half, chunks)),
            pltpu.SemaphoreType.DMA((2, half, chunks)),
            pltpu.SemaphoreType.DMA((ITERS,)),
            pltpu.SemaphoreType.DMA((ITERS,)),
            pltpu.SemaphoreType.DMA((ITERS,)),
            pltpu.SemaphoreType.DMA((ITERS,)),
        ],
        compiler_params=pltpu.CompilerParams(
            collective_id=0, has_side_effects=True, vmem_limit_bytes=48 * 1024 * 1024
        ),
    )(residuals.T, codebook)
    items_scale = items_scale.reshape(rows)
    mixture = lax.psum_scatter(parts, "codes", scatter_dimension=0, tiled=True)
    soft_codes = (mixture * items_scale[None, :]).T
    return soft_codes, items_scale, code_weights.reshape(codes)


def solution(mesh):
    placed = (P("items", "codes"), P("codes", None))
    return jax.shard_map(
        shards,
        mesh=mesh,
        in_specs=placed,
        out_specs=(P("items", "codes"), P("items"), P("codes")),
        check_vma=False,
    )
```

time: 369 us -> 128 us (0.35)
  blocking collectives: 217 us -> 0 us
  Pallas kernels: 0 us -> 68.7 us
  matrix products: 48.5 us -> 0 us
  waiting for transfers between devices: 76.7 us -> 39.9 us
    psum x6 -> x0, blocking collectives: 217 us -> none  [the longest x3 170 us: refresh_right_factors(): return residual_item_count / lax.psum(totals, 'items')]
    pallas_call x0 -> x1, Pallas kernels: none -> 68.7 us  [shards(): pl.pallas_call(functools.partial(kernel, items_n, codes_n, float(rows * i...]
    dot_general x28 -> x0, matrix products: 48.5 us -> none  [the longest x24 39.8 us: kernel_tile(): dots = jnp.dot(rows, codes.T, preferred_element_type=jnp.float32)]
    all_gather x1 -> x0, waiting for transfers between devices: 42.2 us -> none  [shards(): gathered = lax.all_gather(residuals, 'codes', axis=1, tiled=True)]
    reduce_scatter x1, waiting for transfers between devices: 33.8 us -> 39.9 us  [shards(): mixture = lax.psum_scatter(parts, 'codes', scatter_dimension=0, tiled=True)]
  transfers between devices with their start and end apart: 2 -> 1, of which waited for: 2 -> 1; matrix products, arithmetic and copies ran while one was open for 1% -> 0% of each run, Pallas kernels for 0% -> 0%
where the time goes in v1:
time: 128 us; the launch traced here: 127 us
  Pallas kernels  68.7 us (54%)
  waiting for transfers between devices  39.9 us (31%)
  between operations  14 us (11%)
  local copies, waits for them, and re-layouts  3.13 us (2%)
  other arithmetic  1.67 us (1%)
    pallas_call x1, Pallas kernels, shards(): pl.pallas_call(functools.partial(kernel, items_n, codes_n, float(rows * i...  68.7 us
    reduce_scatter x1, waiting for transfers between devices, shards(): mixture = lax.psum_scatter(parts, 'codes', scatter_dimension=0, tiled=True)  39.9 us
    unnamed x6, local copies, waits for them, and re-layouts  3.13 us
  transfers between devices with their start and end apart: 1, of which 1 were waited for; matrix products, arithmetic and copies ran while one was open for 0% of the time, Pallas kernels for 0%

profile of v1, /device:TPU:2, one launch (start us, length us, event | category | flops | bytes accessed | tf_op | source)
XLA Modules:
  0.0 127.4 jit_solution(6770870211579039552)
XLA Ops:
  7.2 0.0 reduce-scatter.2.cloned.1.call-start
  7.2 0.0 copy-start
  7.2 1.0 copy-done
  8.3 0.0 copy-start.1
  8.3 0.9 copy-done.1
  9.2 68.7 %shard_map.49 = (f32[256,2048]{1,0:T(8,128)}, f32[16,128]{1,0:T(8,128)S(1)}, f32[8,128]{1,0:T(8,128)S(1)}) custom-call(bf16[32,2048]{1,0:T(8,128)(2,1)S(1)} %bitcast.5, bf16[1024,256]{1,0:T(8,128)(2,1)S(1)} %copy-done), custom_call_target="tpu_custom_call" | custom-call | tf_op jit(solution)/shard_map/pallas_call | solution.py:222
  77.8 0.0 reduce-scatter.2.cloned.1.call-update
  77.8 39.9 %reduce-scatter.2.cloned.1.call-done = f32[32,2048]{1,0:T(8,128)} async-done(((f32[256,2048]{1,0:T(8,128)}), f32[32,2048]{1,0:T(8,128)}) %reduce-scatter.2.cloned.1.call-update) | async-done | bytes 262160 | tf_op jit(solution)/shard_map/reduce_scatter | solution.py:257
  117.7 1.7 %multiply_bitcast_fusion = f32[2048,32]{0,1:T(8,128)} fusion(f32[32,2048]{1,0:T(8,128)} %reduce-scatter.2.cloned.1.call-done, f32[2048]{0:T(1024)S(1)} %bitcast.6), kind=kLoop, calls=%fused_computation | loop fusion | flops 65536 | bytes 532480 | tf_op jit(solution)/shard_map/transpose | solution.py:258
  119.4 0.6 copy.7
  120.0 0.6 copy.8
Async XLA Ops:
  7.2 110.6 %reduce-scatter.2.cloned.1.call-start = ((), (), s32[]{:S(2)}) async-start(), calls=%async_computation.1 | async-start | bytes 2359296 | tf_op jit(solution)/shard_map/reduce_scatter | solution.py:257
  7.2 1.0 copy-start
  8.3 0.9 copy-start.1
Sparse Core Ops, SparseCore 0:
  78.0 39.7 reduce-scatter.1

commit v2 on v1

v2 whole, which is shorter than its diff:
```python
import functools

import jax
import jax.numpy as jnp
from jax import lax
from jax.experimental import pallas as pl
from jax.experimental.pallas import tpu as pltpu
from jax.sharding import PartitionSpec as P

F = 256
ITERS = 3
EPS = 1e-06
SMOOTHING = 32.0
SHIFT = 2.0
LOG2E = 1.4426950408889634

LANES = 128
CHUNK = 512
TILE = 128
SIDE = 4
MESH = pl.DeviceIdType.MESH


def kernel(
    items_n, codes_n, total_items, total_codes,
    rt_hbm, cb_hbm, soft_ref, s_ref, w_ref,
    cb, cbf, R, K, K2, inv_row, inv_col, tacc, W, tsend, cinv, wbuf, colbuf, rowbuf, sbuf,
    a2, mix, shares, softT, land,
    in_sem, ring_send, ring_recv, col_send, col_recv, row_send, row_recv,
    z_send, z_recv, plane_send, plane_recv, pair_send, pair_recv, out_send, out_recv,
):
    me_i = lax.axis_index("items")
    me_z = lax.axis_index("codes")
    x, y, core = me_i // (2 * SIDE), lax.rem(me_i // 2, SIDE), lax.rem(me_i, 2)
    rows = rt_hbm.shape[1]
    codes = cb_hbm.shape[0]
    feats = rt_hbm.shape[0]
    chunks = rows // CHUNK
    mine = rows // codes_n
    right = lax.rem(me_z + 1, codes_n)
    left = lax.rem(me_z + codes_n - 1, codes_n)
    half = codes_n // 2

    def remote(src, dst, send, recv, device):
        return pltpu.make_async_remote_copy(
            src_ref=src, dst_ref=dst, send_sem=send, recv_sem=recv,
            device_id=device, device_id_type=MESH,
        )

    def wait_bytes(ref, sem):
        pltpu.make_async_copy(ref, ref, sem).wait()

    def at_plane(px, py, pcore):
        return {"items": (px * SIDE + py) * 2 + pcore}

    def block(c, z):
        return R.at[c, pl.ds(pl.multiple_of(z * feats, feats), feats), :]

    own = [
        pltpu.make_async_copy(
            rt_hbm.at[:, c * CHUNK:(c + 1) * CHUNK], block(c, me_z), in_sem.at[c]
        )
        for c in range(chunks)
    ]
    for copy in own:
        copy.start()
    load_cb = pltpu.make_async_copy(cb_hbm, cb, in_sem.at[chunks])
    load_cb.start()

    barrier = pltpu.get_barrier_semaphore()

    def greet_items(k, carry):
        pl.semaphore_signal(
            barrier, inc=1, device_id={"items": lax.rem(me_i + k, items_n)}, device_id_type=MESH
        )
        return carry

    def greet_codes(k, carry):
        pl.semaphore_signal(
            barrier, inc=1, device_id={"codes": lax.rem(me_z + k, codes_n)}, device_id_type=MESH
        )
        return carry

    lax.fori_loop(1, codes_n, greet_codes, 0)
    lax.fori_loop(1, items_n, greet_items, 0)

    load_cb.wait()
    wide = cb[...].astype(jnp.float32)
    inv_col[...] = jnp.broadcast_to(
        lax.rsqrt(jnp.mean(wide * wide, axis=1, keepdims=True) + EPS), inv_col.shape
    )
    for b in range(codes // LANES):
        tsend[b:b + 1, :] = jnp.transpose(inv_col[b * LANES:(b + 1) * LANES, :])[0:1, :]
    cinv[me_z] = tsend[...]
    cbf[me_z, x, y, core] = cb[pl.ds(pl.multiple_of(me_i * 32, 32), 32), :].reshape(2, 16, F)

    pl.semaphore_wait(barrier, items_n + codes_n - 2)

    def hop(direction, h, c):
        z = me_z - (h - 1) if direction == 0 else me_z + (h - 1)
        ref = block(c, lax.rem(z + codes_n, codes_n))
        return remote(
            ref, ref, ring_send.at[direction, h - 1, c], ring_recv.at[direction, h - 1, c],
            {"codes": right if direction == 0 else left},
        )

    def goes(direction, h, c):
        return h < half or (h == half and (c < chunks // 2) == (direction == 0))

    for c in range(chunks):
        own[c].wait()
        for d in range(2):
            if goes(d, 1, c):
                hop(d, 1, c).start()

    def send_codes(k, carry):
        to = {"codes": lax.rem(me_z + k, codes_n)}
        piece = cbf.at[me_z, x, y, core]
        remote(piece, piece, z_send.at[0], z_recv.at[0], to).start()
        remote(cinv.at[me_z], cinv.at[me_z], z_send.at[1], z_recv.at[1], to).start()
        return carry

    lax.fori_loop(1, codes_n, send_codes, 0)

    def plane_copies(stage):
        if stage == 0:
            a, b = cbf.at[:, x, y, core, 0], cbf.at[:, x, y, core, 1]
        else:
            b, a = cbf.at[:, :, y, core, 0], cbf.at[:, x, :, core, 1]
        out = []
        for k in range(1, SIDE):
            to_x = at_plane(lax.rem(x + k, SIDE), y, core)
            to_y = at_plane(x, lax.rem(y + k, SIDE), core)
            out.append(remote(a, a, plane_send.at[stage, 0], plane_recv.at[stage, 0], to_x))
            out.append(remote(b, b, plane_send.at[stage, 1], plane_recv.at[stage, 1], to_y))
        return out

    def plane_wait(stage, sem):
        for way in range(2):
            if stage == 0:
                ref = cbf.at[:, 0, pl.ds(0, SIDE - 1), 0, 0]
            else:
                ref = cbf.at[:, :, pl.ds(0, SIDE - 1), 0, 0]
            wait_bytes(ref, sem.at[stage, way])

    def pair_copy():
        ref = cbf.at[:, :, :, core]
        return remote(ref, ref, pair_send, pair_recv, at_plane(x, y, 1 - core))

    for h in range(1, half + 1):
        for c in range(chunks):
            for d in range(2):
                if goes(d, h, c):
                    hop(d, h, c).wait_recv()
                    if goes(d, h + 1, c):
                        hop(d, h + 1, c).start()
        if h == 2:
            wait_bytes(cbf.at[pl.ds(0, codes_n - 1), 0, 0, 0], z_recv.at[0])
            wait_bytes(cinv.at[pl.ds(0, codes_n - 1)], z_recv.at[1])
            for copy in plane_copies(0):
                copy.start()

    plane_wait(0, plane_recv)
    for copy in plane_copies(1):
        copy.start()

    tacc[...] = jnp.zeros_like(tacc)
    for c in range(chunks):
        r_wide = R[c].astype(jnp.float32)
        inv_row[...] = lax.rsqrt(
            jnp.mean(r_wide * r_wide, axis=0, keepdims=True) + EPS
        ) * (SMOOTHING * LOG2E / F)

        def tile_step(m, carry, c=c):
            at = pl.ds(pl.multiple_of(m * TILE, TILE), TILE)
            dots = jnp.dot(cb[at, :], R[c], preferred_element_type=jnp.float32)
            scale = inv_col[at, :]
            total = tacc[at, :]
            for q in range(CHUNK // LANES):
                lanes = slice(q * LANES, (q + 1) * LANES)
                value = jnp.exp2(dots[:, lanes] * inv_row[:, lanes] * scale - SHIFT * LOG2E)
                K[at, c * CHUNK + q * LANES:c * CHUNK + (q + 1) * LANES] = value
                total = total + value
            tacc[at, :] = total
            return carry

        lax.fori_loop(0, codes // TILE, tile_step, 0)

    groups = codes // 8
    lane_chunks = rows // LANES

    def exchange(buf, mine_at, count, axis, send_sem, recv_sem):
        def send(k, carry):
            ref = buf.at[mine_at]
            remote(ref, ref, send_sem, recv_sem, {axis: lax.rem(mine_at + k, count)}).start()
            return carry

        lax.fori_loop(1, count, send, 0)

    def all_but_one(buf, count, sem):
        wait_bytes(buf.at[pl.ds(0, count - 1)], sem)

    def second_tile():
        my_rows = R[me_z // (CHUNK // mine), :, pl.ds(
            pl.multiple_of(lax.rem(me_z, CHUNK // mine) * mine, mine), mine)]
        rows2 = jnp.transpose(my_rows)
        wide2 = rows2.astype(jnp.float32)
        a2[...] = jnp.broadcast_to(
            lax.rsqrt(jnp.mean(wide2 * wide2, axis=1, keepdims=True) + EPS)
            * (SMOOTHING * LOG2E / F), a2.shape)
        softT[...] = wide2

        def step(n, carry):
            z, k = n // 4, lax.rem(n, 4)
            some = cbf[z, k].reshape(codes // 4, F)
            dots = lax.dot_general(
                softT[...].astype(jnp.bfloat16), some, (((1,), (1,)), ((), ())),
                preferred_element_type=jnp.float32,
            )
            for q in range(2):
                scale = cinv[z, pl.ds(2 * k + q, 1), :]
                value = jnp.exp2(
                    dots[:, q * LANES:(q + 1) * LANES] * a2[...] * scale - SHIFT * LOG2E)
                K2[:, pl.ds(pl.multiple_of(n * 256 + q * LANES, LANES), LANES)] = value
            return carry

        lax.fori_loop(0, codes_n * 4, step, 0)

    for it in range(ITERS):
        last = it == ITERS - 1
        if it > 0:
            s_bcast = [
                jnp.broadcast_to(s_ref[q:q + 1, :], (8, LANES)) for q in range(lane_chunks)
            ]

            def col_step(g, carry):
                at = pl.ds(pl.multiple_of(g * 8, 8), 8)
                total = K[at, 0:LANES] * s_bcast[0]
                for q in range(1, lane_chunks):
                    total = total + K[at, q * LANES:(q + 1) * LANES] * s_bcast[q]
                tacc[at, :] = total
                return carry

            lax.fori_loop(0, groups, col_step, 0, unroll=4)
        for b in range(codes // LANES):
            blockT = jnp.transpose(tacc[b * LANES:(b + 1) * LANES, :])
            tsend[b:b + 1, :] = jnp.sum(blockT, axis=0, keepdims=True)
        colbuf[it, me_i] = tsend[...]
        exchange(colbuf.at[it], me_i, items_n, "items", col_send.at[it], col_recv.at[it])
        if it == 1:
            plane_wait(1, plane_recv)
            pair_copy().start()
        if last:
            pair_copy().wait_recv()
            second_tile()
        all_but_one(colbuf.at[it], items_n, col_recv.at[it])
        w = total_items / jnp.sum(colbuf[it], axis=0)
        if last:
            w_ref[...] = w
            wbuf[me_z] = w * (1.0 / total_codes)
            exchange(wbuf, me_z, codes_n, "codes", row_send.at[it], row_recv.at[it])
            all_but_one(wbuf, codes_n, row_recv.at[it])
            break
        for b in range(codes // LANES):
            W[b * LANES:(b + 1) * LANES, :] = jnp.transpose(
                jnp.broadcast_to(w[b:b + 1, :], (LANES, LANES))
            )

        def row_step(g, acc):
            at = pl.ds(pl.multiple_of(g * 8, 8), 8)
            weight = W[at, :]
            return tuple(
                acc[q] + K[at, q * LANES:(q + 1) * LANES] * weight for q in range(lane_chunks)
            )

        acc = lax.fori_loop(
            0, groups, row_step,
            tuple(jnp.zeros((8, LANES), jnp.float32) for _ in range(lane_chunks)), unroll=4,
        )
        for q in range(lane_chunks):
            s_ref[q:q + 1, :] = jnp.sum(acc[q], axis=0, keepdims=True)
        rowbuf[it, me_z] = s_ref[...]
        exchange(rowbuf.at[it], me_z, codes_n, "codes", row_send.at[it], row_recv.at[it])
        all_but_one(rowbuf.at[it], codes_n, row_recv.at[it])
        s_ref[...] = total_codes / jnp.sum(rowbuf[it], axis=0)

    mix[...] = jnp.zeros_like(mix)
    a2[...] = jnp.zeros_like(a2)

    def soft_step(z, carry):
        total = a2[...]
        for q in range(codes // LANES):
            value = K2[:, pl.ds(pl.multiple_of(z * codes + q * LANES, LANES), LANES)]
            value = value * wbuf[z, pl.ds(q, 1), :]
            total = total + value
            shares[:, q * LANES:(q + 1) * LANES] = value.astype(jnp.bfloat16)
        a2[...] = total
        mix[...] += jnp.dot(
            shares[...], cbf[z].reshape(codes, F), preferred_element_type=jnp.float32
        )
        return carry

    lax.fori_loop(0, codes_n, soft_step, 0)
    for b in range(mine // LANES):
        at = slice(b * LANES, (b + 1) * LANES)
        scale = 1.0 / jnp.sum(jnp.transpose(a2[at, :]), axis=0, keepdims=True)
        sbuf[me_z, b:b + 1, :] = scale
        softT[:, at] = jnp.transpose(mix[at, :]) * scale

    def part(z):
        return pl.ds(pl.multiple_of(z * feats, feats), feats)

    my_lanes = pl.ds(pl.multiple_of(me_z * mine, mine), mine)

    def send_out(k, carry):
        z = lax.rem(me_z + k, codes_n)
        remote(softT.at[part(z), :], land.at[:, my_lanes], out_send.at[0], out_recv.at[0],
               {"codes": z}).start()
        remote(sbuf.at[me_z], sbuf.at[me_z], out_send.at[1], out_recv.at[1],
               {"codes": z}).start()
        return carry

    lax.fori_loop(1, codes_n, send_out, 0)
    land[:, my_lanes] = softT[part(me_z), :]
    sent = land.at[:, pl.ds(0, (codes_n - 1) * mine)]
    some = sbuf.at[pl.ds(0, codes_n - 1)]
    wait_bytes(sent, out_recv.at[0])
    wait_bytes(some, out_recv.at[1])
    soft_ref[...] = land[...]
    for z in range(codes_n):
        for b in range(mine // LANES):
            n = z * (mine // LANES) + b
            s_ref[n:n + 1, :] = sbuf[z, b:b + 1, :]

    wait_bytes(sent, out_send.at[0])
    wait_bytes(some, out_send.at[1])
    for it in range(ITERS):
        all_but_one(colbuf.at[it], items_n, col_send.at[it])
        if it < ITERS - 1:
            all_but_one(rowbuf.at[it], codes_n, row_send.at[it])
        else:
            all_but_one(wbuf, codes_n, row_send.at[it])
    wait_bytes(cbf.at[pl.ds(0, codes_n - 1), 0, 0, 0], z_send.at[0])
    wait_bytes(cinv.at[pl.ds(0, codes_n - 1)], z_send.at[1])
    plane_wait(0, plane_send)
    plane_wait(1, plane_send)
    pair_copy().wait_send()
    for h in range(1, half + 1):
        for c in range(chunks):
            for d in range(2):
                if goes(d, h, c):
                    hop(d, h, c).wait_send()


def shards(residuals, codebook):
    items_n, codes_n = lax.axis_size("items"), lax.axis_size("codes")
    rows, feats = residuals.shape
    codes = codebook.shape[0]
    chunks = rows // CHUNK
    half = codes_n // 2
    mine = rows // codes_n
    f32, bf16 = jnp.float32, jnp.bfloat16
    hbm = pl.BlockSpec(memory_space=pltpu.HBM)
    vmem = pl.BlockSpec(memory_space=pltpu.VMEM)
    dma = pltpu.SemaphoreType.DMA
    softT, items_scale, code_weights = pl.pallas_call(
        functools.partial(
            kernel, items_n, codes_n, float(rows * items_n), float(codes * codes_n)
        ),
        out_shape=(
            jax.ShapeDtypeStruct((feats, rows), f32),
            jax.ShapeDtypeStruct((rows // LANES, LANES), f32),
            jax.ShapeDtypeStruct((codes // LANES, LANES), f32),
        ),
        in_specs=[hbm, hbm],
        out_specs=(vmem, vmem, vmem),
        scratch_shapes=[
            pltpu.VMEM((codes, F), bf16),
            pltpu.VMEM((codes_n, SIDE, SIDE, 2, 2, 16, F), bf16),
            pltpu.VMEM((chunks, F, CHUNK), bf16),
            pltpu.VMEM((codes, rows), f32),
            pltpu.VMEM((mine, codes * codes_n), f32),
            pltpu.VMEM((1, CHUNK), f32),
            pltpu.VMEM((codes, LANES), f32),
            pltpu.VMEM((codes, LANES), f32),
            pltpu.VMEM((codes, LANES), f32),
            pltpu.VMEM((codes // LANES, LANES), f32),
            pltpu.VMEM((codes_n, codes // LANES, LANES), f32),
            pltpu.VMEM((codes_n, codes // LANES, LANES), f32),
            pltpu.VMEM((ITERS, items_n, codes // LANES, LANES), f32),
            pltpu.VMEM((ITERS - 1, codes_n, rows // LANES, LANES), f32),
            pltpu.VMEM((codes_n, mine // LANES, LANES), f32),
            pltpu.VMEM((mine, LANES), f32),
            pltpu.VMEM((mine, F), f32),
            pltpu.VMEM((mine, codes), bf16),
            pltpu.VMEM((F, mine), f32),
            pltpu.VMEM((feats, rows), f32),
            dma((chunks + 1,)),
            dma((2, half, chunks)),
            dma((2, half, chunks)),
            dma((ITERS,)), dma((ITERS,)), dma((ITERS,)), dma((ITERS,)),
            dma((2,)), dma((2,)),
            dma((2, 2)), dma((2, 2)),
            dma, dma,
            dma((2,)), dma((2,)),
        ],
        compiler_params=pltpu.CompilerParams(
            collective_id=0, has_side_effects=True, vmem_limit_bytes=48 * 1024 * 1024
        ),
    )(residuals.T, codebook)
    return softT.T, items_scale.reshape(rows), code_weights.reshape(codes)


def solution(mesh):
    placed = (P("items", "codes"), P("codes", None))
    return jax.shard_map(
        shards,
        mesh=mesh,
        in_specs=placed,
        out_specs=(P("items", "codes"), P("items"), P("codes")),
        check_vma=False,
    )
```

time: 128 us -> 90.7 us (0.71)
  waiting for transfers between devices: 39.9 us -> 0 us
  Pallas kernels: 68.7 us -> 85.7 us
  between operations: 14 us -> 0.65 us
  other arithmetic: 1.67 us -> 0 us
    reduce_scatter x1 -> x0, waiting for transfers between devices: 39.9 us -> none  [shards(): mixture = lax.psum_scatter(parts, 'codes', scatter_dimension=0, tiled=True)]
    pallas_call x1, Pallas kernels: 68.7 us -> 85.7 us  [shards(): pl.pallas_call(functools.partial(kernel, items_n, codes_n, float(rows * i...]
    transpose x1 -> x0, other arithmetic: 1.67 us -> none  [shards(): soft_codes = (mixture * items_scale[None, :]).T]
    unnamed x6 -> x7, local copies, waits for them, and re-layouts: 3.13 us -> 3.84 us
  transfers between devices with their start and end apart: 1 -> 0, of which waited for: 1 -> 0; matrix products, arithmetic and copies ran while one was open for 0% -> 0% of each run, Pallas kernels for 0% -> 0%
where the time goes in v2:
time: 90.7 us; the launch traced here: 90.2 us
  Pallas kernels  85.7 us (94%)
  local copies, waits for them, and re-layouts  3.84 us (4%)
    pallas_call x1, Pallas kernels, shards(): pl.pallas_call(functools.partial(kernel, items_n, codes_n, float(rows * i...  85.7 us
    unnamed x7, local copies, waits for them, and re-layouts  3.84 us

profile of v2, /device:TPU:2, one launch (start us, length us, event | category | flops | bytes accessed | tf_op | source)
XLA Modules:
  0.0 90.2 jit_solution(17474201606127823137)
XLA Ops:
  0.6 0.0 copy-start
  0.6 1.0 %copy-done = bf16[1024,256]{1,0:T(8,128)(2,1)S(1)} copy-done((bf16[1024,256]{1,0:T(8,128)(2,1)S(1)}, bf16[1024,256]{1,0:T(8,128)(2,1)}, u32[]{:S(2)}) %copy-start) | copy-done | bytes 524312
  1.7 0.0 copy-start.1
  1.7 0.9 %copy-done.1 = bf16[2048,32]{0,1:T(8,128)(2,1)S(1)} copy-done((bf16[2048,32]{0,1:T(8,128)(2,1)S(1)}, bf16[2048,32]{0,1:T(8,128)(2,1)}, u32[]{:S(2)}) %copy-start.1) | copy-done | bytes 131096
  2.6 85.7 %shard_map.49 = (f32[32,2048]{1,0:T(8,128)S(1)}, f32[16,128]{1,0:T(8,128)S(1)}, f32[8,128]{1,0:T(8,128)S(1)}) custom-call(bf16[32,2048]{1,0:T(8,128)(2,1)S(1)} %bitcast.5, bf16[1024,256]{1,0:T(8,128)(2,1)S(1)} %copy-done), custom_call_target="tpu_custom_call" | custom-call | tf_op jit(solution)/shard_map/pallas_call | solution.py:366
  88.3 0.7 copy.8
  89.0 0.6 copy.9
  89.6 0.6 copy.10
Async XLA Ops:
  0.6 1.0 %copy-start = (bf16[1024,256]{1,0:T(8,128)(2,1)S(1)}, bf16[1024,256]{1,0:T(8,128)(2,1)}, u32[]{:S(2)}) copy-start(bf16[1024,256]{1,0:T(8,128)(2,1)} %cb_hbm.1) | copy-start | bytes 1572868
  1.7 0.9 %copy-start.1 = (bf16[2048,32]{0,1:T(8,128)(2,1)S(1)}, bf16[2048,32]{0,1:T(8,128)(2,1)}, u32[]{:S(2)}) copy-start(bf16[2048,32]{0,1:T(8,128)(2,1)} %param.2) | copy-start | bytes 393220

commit v3 on v2

v3 whole, which is shorter than its diff:
```python
import functools
import math

import jax
import jax.numpy as jnp
from jax import lax
from jax.experimental import pallas as pl
from jax.experimental.pallas import tpu as pltpu
from jax.sharding import PartitionSpec as P

F = 256
ITERS = 3
EPS = 1e-06
SMOOTHING = 32.0
SHIFT = 2.0
LOG2E = 1.4426950408889634

LANES = 128
CHUNK = 256
TILE = 256
PARTS = 4
VMEM_BYTES = 48 * 1024 * 1024
SIDE = 4
MESH = pl.DeviceIdType.MESH


def ring_plan(codes_n, units):
    half = codes_n // 2

    def goes(d, h, u):
        return h < half or (h == half and (u % 2 == 0) == (d == 0))

    return [
        (d, h, u, goes(d, h + 1, u))
        for h in range(1, half + 1) for u in range(units) for d in range(2) if goes(d, h, u)
    ]


def tree_sum(terms):
    while len(terms) > 1:
        terms = [a + b for a, b in zip(terms[::2], terms[1::2])] + terms[len(terms) // 2 * 2:]
    return terms[0]


def kernel(
    items_n, codes_n, total_items, total_codes,
    rt_hbm, cb_hbm, soft_ref, s_ref, w_ref,
    cb, cbf, R, K, K2, inv_row, inv_col, tacc, W, tsend, cinv, wbuf, colbuf, rowbuf, sbuf,
    rows2, a2, r2, mix, shares_a, shares_b, softT, land,
    in_sem, ring_send, ring_recv, col_send, col_recv, row_send, row_recv,
    z_send, z_recv, plane_send, plane_recv, pair_send, pair_recv, out_send, out_recv,
):
    me_i = lax.axis_index("items")
    me_z = lax.axis_index("codes")
    x, y, core = me_i // (2 * SIDE), lax.rem(me_i // 2, SIDE), lax.rem(me_i, 2)
    rows = rt_hbm.shape[1]
    codes = cb_hbm.shape[0]
    feats = rt_hbm.shape[0]
    chunks = rows // CHUNK
    mine = rows // codes_n
    right = lax.rem(me_z + 1, codes_n)
    left = lax.rem(me_z + codes_n - 1, codes_n)
    half = codes_n // 2

    def remote(src, dst, send, recv, device):
        return pltpu.make_async_remote_copy(
            src_ref=src, dst_ref=dst, send_sem=send, recv_sem=recv,
            device_id=device, device_id_type=MESH,
        )

    def wait_bytes(ref, sem):
        pltpu.make_async_copy(ref, ref, sem).wait()

    def at_plane(px, py, pcore):
        return {"items": (px * SIDE + py) * 2 + pcore}

    def block(c, z):
        return R.at[c, pl.ds(pl.multiple_of(z * feats, feats), feats), :]

    own = [
        pltpu.make_async_copy(
            rt_hbm.at[:, c * CHUNK:(c + 1) * CHUNK], block(c, me_z), in_sem.at[c]
        )
        for c in range(chunks)
    ]
    own += [
        pltpu.make_async_copy(
            cb_hbm.at[pl.ds(pl.multiple_of(me_i * 32 + n * 16, 16), 16), :],
            cbf.at[me_z, x, y, core, n], in_sem.at[chunks + 1 + n],
        )
        for n in range(2)
    ]
    for copy in own:
        copy.start()
    load_cb = pltpu.make_async_copy(cb_hbm, cb, in_sem.at[chunks])
    load_cb.start()

    barrier = pltpu.get_barrier_semaphore()

    def greet_items(k, carry):
        pl.semaphore_signal(
            barrier, inc=1, device_id={"items": lax.rem(me_i + k, items_n)}, device_id_type=MESH
        )
        return carry

    def greet_codes(k, carry):
        pl.semaphore_signal(
            barrier, inc=1, device_id={"codes": lax.rem(me_z + k, codes_n)}, device_id_type=MESH
        )
        return carry

    lax.fori_loop(1, codes_n, greet_codes, 0)
    lax.fori_loop(1, items_n, greet_items, 0)

    pl.semaphore_wait(barrier, items_n + codes_n - 2)

    def hop(direction, h, u):
        z = me_z - (h - 1) if direction == 0 else me_z + (h - 1)
        z = lax.rem(z + codes_n, codes_n)
        ref = cbf.at[z, x, y, core] if u == 0 else block(u - 1, z)
        return remote(
            ref, ref, ring_send.at[direction, h - 1, u], ring_recv.at[direction, h - 1, u],
            {"codes": right if direction == 0 else left},
        )

    for copy in own:
        copy.wait()
    for u in range(chunks + 1):
        for d in range(2):
            hop(d, 1, u).start()
    load_cb.wait()
    wide = cb[...].astype(jnp.float32)
    inv_col[...] = jnp.broadcast_to(
        lax.rsqrt(jnp.mean(wide * wide, axis=1, keepdims=True) + EPS), inv_col.shape
    )
    for b in range(codes // LANES):
        tsend[b:b + 1, :] = jnp.transpose(inv_col[b * LANES:(b + 1) * LANES, :])[0:1, :]
    cinv[me_z] = tsend[...]

    def plane_copies(part):
        if part == 0:
            a, b = cbf.at[:, x, y, core, 0], cbf.at[:, x, y, core, 1]
        else:
            zs = pl.ds((part - 1) * (codes_n // PARTS), codes_n // PARTS)
            b, a = cbf.at[zs, :, y, core, 0], cbf.at[zs, x, :, core, 1]
        out = []
        for k in range(1, SIDE):
            to_x = at_plane(lax.rem(x + k, SIDE), y, core)
            to_y = at_plane(x, lax.rem(y + k, SIDE), core)
            out.append(remote(a, a, plane_send.at[part, 0], plane_recv.at[part, 0], to_x))
            out.append(remote(b, b, plane_send.at[part, 1], plane_recv.at[part, 1], to_y))
        return out

    def plane_start(part):
        for copy in plane_copies(part):
            copy.start()

    def plane_wait(part, sem):
        for way in range(2):
            if part == 0:
                ref = cbf.at[:, 0, pl.ds(0, SIDE - 1), 0, 0]
            else:
                ref = cbf.at[pl.ds(0, codes_n // PARTS), :, pl.ds(0, SIDE - 1), 0, 0]
            wait_bytes(ref, sem.at[part, way])

    def pair_copy(part):
        ref = cbf.at[pl.ds(part * (codes_n // PARTS), codes_n // PARTS), :, :, core]
        return remote(ref, ref, pair_send.at[part], pair_recv.at[part], at_plane(x, y, 1 - core))

    def tile(c):
        r_wide = R[c].astype(jnp.float32)
        inv_row[...] = lax.rsqrt(
            jnp.mean(r_wide * r_wide, axis=0, keepdims=True) + EPS
        ) * (SMOOTHING * LOG2E / F)

        def tile_step(m, carry):
            at = pl.ds(pl.multiple_of(m * TILE, TILE), TILE)
            dots = jnp.dot(cb[at, :], R[c], preferred_element_type=jnp.float32)
            scale = inv_col[at, :]
            values = []
            for q in range(CHUNK // LANES):
                lanes = slice(q * LANES, (q + 1) * LANES)
                value = jnp.exp2(dots[:, lanes] * inv_row[:, lanes] * scale)
                K[at, c * CHUNK + q * LANES:c * CHUNK + (q + 1) * LANES] = value
                values.append(value)
            total = tree_sum(values)
            if c in first_tile:
                tacc[at, :] = total
            else:
                tacc[at, :] += total
            return carry

        lax.fori_loop(0, codes // TILE, tile_step, 0, unroll=True)

    plan = ring_plan(codes_n, chunks + 1)
    left_over = [sum(1 for d, h, u, then in plan if u == v) for v in range(chunks + 1)]
    first_tile = []
    for d, h, u, then in plan:
        hop(d, h, u).wait_recv()
        if then:
            hop(d, h + 1, u).start()
        left_over[u] -= 1
        if left_over[u] == 0:
            if u == 0:
                plane_start(0)
            else:
                if not first_tile:
                    first_tile.append(u - 1)
                else:
                    first_tile[:] = [-1]
                tile(u - 1)

    groups = codes // 8
    lane_chunks = rows // LANES

    def exchange(buf, mine_at, count, axis, send_sem, recv_sem):
        def send(k, carry):
            ref = buf.at[mine_at]
            remote(ref, ref, send_sem, recv_sem, {axis: lax.rem(mine_at + k, count)}).start()
            return carry

        lax.fori_loop(1, count, send, 0)

    def all_but_one(buf, count, sem):
        wait_bytes(buf.at[pl.ds(0, count - 1)], sem)

    def second_rows():
        rows2[...] = jnp.transpose(R[me_z])
        wide2 = rows2[...].astype(jnp.float32)
        a2[...] = jnp.broadcast_to(
            lax.rsqrt(jnp.mean(wide2 * wide2, axis=1, keepdims=True) + EPS)
            * (SMOOTHING * LOG2E / F), a2.shape)

    def second_tile(part):
        def step(n, carry):
            z, k = n // 4, lax.rem(n, 4)
            some = cbf[z, k].reshape(codes // 4, F)
            dots = lax.dot_general(
                rows2[...], some, (((1,), (1,)), ((), ())), preferred_element_type=jnp.float32
            )
            for q in range(2):
                scale = cinv[z, pl.ds(2 * k + q, 1), :]
                value = jnp.exp2(dots[:, q * LANES:(q + 1) * LANES] * a2[...] * scale)
                K2[:, pl.ds(pl.multiple_of(n * 256 + q * LANES, LANES), LANES)] = value
            return carry

        steps = 4 * codes_n // PARTS
        lax.fori_loop(part * steps, (part + 1) * steps, step, 0, unroll=4)

    def send_inv(k, carry):
        remote(cinv.at[me_z], cinv.at[me_z], z_send, z_recv,
               {"codes": lax.rem(me_z + k, codes_n)}).start()
        return carry

    lax.fori_loop(1, codes_n, send_inv, 0)

    for it in range(ITERS):
        last = it == ITERS - 1
        if it > 0:
            s_bcast = [
                jnp.broadcast_to(s_ref[q:q + 1, :], (8, LANES)) for q in range(lane_chunks)
            ]

            def col_step(g, carry):
                at = pl.ds(pl.multiple_of(g * 8, 8), 8)
                tacc[at, :] = tree_sum([
                    K[at, q * LANES:(q + 1) * LANES] * s_bcast[q] for q in range(lane_chunks)
                ])
                return carry

            lax.fori_loop(0, groups, col_step, 0, unroll=4)
        for b in range(codes // LANES):
            blockT = jnp.transpose(tacc[b * LANES:(b + 1) * LANES, :])
            tsend[b:b + 1, :] = jnp.sum(blockT, axis=0, keepdims=True)
        colbuf[it, me_i] = tsend[...]
        exchange(colbuf.at[it], me_i, items_n, "items", col_send.at[it], col_recv.at[it])
        if it == 0:
            for d, h, u, then in plan:
                hop(d, h, u).wait_send()
            second_rows()
            plane_wait(0, plane_recv)
        if it == 1:
            for part in (0, 1):
                plane_wait(1 + part, plane_recv)
                pair_copy(part).start()
            plane_wait(0, plane_send)
            all_but_one(colbuf.at[0], items_n, col_send.at[0])
            all_but_one(rowbuf.at[0], codes_n, row_send.at[0])
            all_but_one(cinv, codes_n, z_recv)
            all_but_one(cinv, codes_n, z_send)
        if last:
            for part in (2, 3):
                plane_wait(1 + part, plane_recv)
                pair_copy(part).start()
            for part in (2, 3):
                pair_copy(part).wait_recv()
                second_tile(part)
        all_but_one(colbuf.at[it], items_n, col_recv.at[it])
        if not last:
            plane_start(1 + 2 * it)
            plane_start(2 + 2 * it)
        w = total_items / jnp.sum(colbuf[it], axis=0)
        if last:
            w_ref[...] = w * math.exp(SHIFT)
            wbuf[me_z] = w * (1.0 / total_codes)
            exchange(wbuf, me_z, codes_n, "codes", row_send.at[it], row_recv.at[it])
            for past in (1, 2):
                all_but_one(colbuf.at[past], items_n, col_send.at[past])
            all_but_one(rowbuf.at[1], codes_n, row_send.at[1])
            for part in range(PARTS):
                plane_wait(1 + part, plane_send)
                pair_copy(part).wait_send()
            all_but_one(wbuf, codes_n, row_recv.at[it])
            break
        for b in range(codes // LANES):
            W[b * LANES:(b + 1) * LANES, :] = jnp.transpose(
                jnp.broadcast_to(w[b:b + 1, :], (LANES, LANES))
            )

        def row_step(g, acc):
            at = pl.ds(pl.multiple_of(g * 8, 8), 8)
            weight = W[at, :]
            return tuple(
                acc[q] + K[at, q * LANES:(q + 1) * LANES] * weight for q in range(lane_chunks)
            )

        acc = lax.fori_loop(
            0, groups, row_step,
            tuple(jnp.zeros((8, LANES), jnp.float32) for _ in range(lane_chunks)), unroll=4,
        )
        for q in range(lane_chunks):
            s_ref[q:q + 1, :] = jnp.sum(acc[q], axis=0, keepdims=True)
        rowbuf[it, me_z] = s_ref[...]
        exchange(rowbuf.at[it], me_z, codes_n, "codes", row_send.at[it], row_recv.at[it])
        if it == 1:
            for part in (0, 1):
                pair_copy(part).wait_recv()
                second_tile(part)
        all_but_one(rowbuf.at[it], codes_n, row_recv.at[it])
        s_ref[...] = total_codes / jnp.sum(rowbuf[it], axis=0)

    def part_of(z):
        return pl.ds(pl.multiple_of(z * feats, feats), feats)

    def shares_of(z, at, out):
        total = []
        for q in range(codes // LANES):
            value = K2[at, z * codes + q * LANES:z * codes + (q + 1) * LANES] * wbuf[z, q:q + 1, :]
            total.append(value)
            out[:, q * LANES:(q + 1) * LANES] = value.astype(jnp.bfloat16)
        r2[...] = tree_sum(total) if z == 0 else r2[...] + tree_sum(total)

    def mix_of(z, src):
        some = jnp.dot(src[...], cbf[z].reshape(codes, F), preferred_element_type=jnp.float32)
        mix[...] = some if z == 0 else mix[...] + some

    buffers = (shares_a, shares_b)
    for b in range(mine // LANES):
        at = slice(b * LANES, (b + 1) * LANES)
        shares_of(0, at, buffers[0])
        for z in range(codes_n):
            if z + 1 < codes_n:
                shares_of(z + 1, at, buffers[(z + 1) % 2])
            mix_of(z, buffers[z % 2])
        scale = 1.0 / jnp.sum(jnp.transpose(r2[...]), axis=0, keepdims=True)
        sbuf[me_z, b:b + 1, :] = scale
        softT[b] = jnp.transpose(mix[...]) * scale
        my_lanes = pl.ds(pl.multiple_of(me_z * mine + b * LANES, LANES), LANES)

        def send_out(k, carry, b=b, my_lanes=my_lanes):
            z = lax.rem(me_z + k, codes_n)
            remote(softT.at[b, part_of(z), :], land.at[:, my_lanes],
                   out_send.at[b], out_recv.at[b], {"codes": z}).start()
            return carry

        lax.fori_loop(1, codes_n, send_out, 0)
        land[:, my_lanes] = softT[b, part_of(me_z), :]
    exchange(sbuf, me_z, codes_n, "codes", out_send.at[2], out_recv.at[2])
    all_but_one(wbuf, codes_n, row_send.at[ITERS - 1])

    for b in range(mine // LANES):
        wait_bytes(land.at[:, pl.ds(0, (codes_n - 1) * LANES)], out_recv.at[b])
    all_but_one(sbuf, codes_n, out_recv.at[2])
    soft_ref[...] = land[...]
    for z in range(codes_n):
        for b in range(mine // LANES):
            n = z * (mine // LANES) + b
            s_ref[n:n + 1, :] = sbuf[z, b:b + 1, :]
    for b in range(mine // LANES):
        wait_bytes(land.at[:, pl.ds(0, (codes_n - 1) * LANES)], out_send.at[b])
    all_but_one(sbuf, codes_n, out_send.at[2])


def shards(residuals, codebook):
    items_n, codes_n = lax.axis_size("items"), lax.axis_size("codes")
    rows, feats = residuals.shape
    codes = codebook.shape[0]
    chunks = rows // CHUNK
    half = codes_n // 2
    mine = rows // codes_n
    f32, bf16 = jnp.float32, jnp.bfloat16
    hbm = pl.BlockSpec(memory_space=pltpu.HBM)
    vmem = pl.BlockSpec(memory_space=pltpu.VMEM)
    dma = pltpu.SemaphoreType.DMA
    softT, items_scale, code_weights = pl.pallas_call(
        functools.partial(
            kernel, items_n, codes_n, float(rows * items_n), float(codes * codes_n)
        ),
        out_shape=(
            jax.ShapeDtypeStruct((feats, rows), f32),
            jax.ShapeDtypeStruct((rows // LANES, LANES), f32),
            jax.ShapeDtypeStruct((codes // LANES, LANES), f32),
        ),
        in_specs=[hbm, hbm],
        out_specs=(vmem, vmem, vmem),
        scratch_shapes=[
            pltpu.VMEM((codes, F), bf16),
            pltpu.VMEM((codes_n, SIDE, SIDE, 2, 2, 16, F), bf16),
            pltpu.VMEM((chunks, F, CHUNK), bf16),
            pltpu.VMEM((codes, rows), f32),
            pltpu.VMEM((mine, codes * codes_n), f32),
            pltpu.VMEM((1, CHUNK), f32),
            pltpu.VMEM((codes, LANES), f32),
            pltpu.VMEM((codes, LANES), f32),
            pltpu.VMEM((codes, LANES), f32),
            pltpu.VMEM((codes // LANES, LANES), f32),
            pltpu.VMEM((codes_n, codes // LANES, LANES), f32),
            pltpu.VMEM((codes_n, codes // LANES, LANES), f32),
            pltpu.VMEM((ITERS, items_n, codes // LANES, LANES), f32),
            pltpu.VMEM((ITERS - 1, codes_n, rows // LANES, LANES), f32),
            pltpu.VMEM((codes_n, mine // LANES, LANES), f32),
            pltpu.VMEM((mine, F), bf16),
            pltpu.VMEM((mine, LANES), f32),
            pltpu.VMEM((LANES, LANES), f32),
            pltpu.VMEM((LANES, F), f32),
            pltpu.VMEM((LANES, codes), bf16),
            pltpu.VMEM((LANES, codes), bf16),
            pltpu.VMEM((mine // LANES, F, LANES), f32),
            pltpu.VMEM((feats, rows), f32),
            dma((chunks + 3,)),
            dma((2, half, chunks + 1)),
            dma((2, half, chunks + 1)),
            dma((ITERS,)), dma((ITERS,)), dma((ITERS,)), dma((ITERS,)),
            dma, dma,
            dma((PARTS + 1, 2)), dma((PARTS + 1, 2)),
            dma((PARTS,)), dma((PARTS,)),
            dma((3,)), dma((3,)),
        ],
        compiler_params=pltpu.CompilerParams(
            collective_id=0, has_side_effects=True, vmem_limit_bytes=VMEM_BYTES
        ),
    )(pltpu.with_memory_space_constraint(residuals.T, pltpu.HBM), pltpu.with_memory_space_constraint(codebook, pltpu.HBM))
    return softT.T, items_scale.reshape(rows), code_weights.reshape(codes)


def solution(mesh):
    placed = (P("items", "codes"), P("codes", None))
    return jax.shard_map(
        shards,
        mesh=mesh,
        in_specs=placed,
        out_specs=(P("items", "codes"), P("items"), P("codes")),
        check_vma=False,
    )
```

time: 90.7 us -> 74.6 us (0.82)
  Pallas kernels: 85.7 us -> 70.7 us
  local copies, waits for them, and re-layouts: 3.84 us -> 1.9 us
    pallas_call x1, Pallas kernels: 85.7 us -> 70.7 us  [shards(): pl.pallas_call(functools.partial(kernel, items_n, codes_n, float(rows * i...]
    unnamed x7 -> x3, local copies, waits for them, and re-layouts: 3.84 us -> 1.9 us
where the time goes in v3:
time: 74.6 us; the launch traced here: 73.2 us
  Pallas kernels  70.7 us (95%)
  local copies, waits for them, and re-layouts  1.9 us (3%)
    pallas_call x1, Pallas kernels, shards(): pl.pallas_call(functools.partial(kernel, items_n, codes_n, float(rows * i...  70.7 us
    unnamed x3, local copies, waits for them, and re-layouts  1.9 us

profile of v3, /device:TPU:2, one launch (start us, length us, event | category | flops | bytes accessed | tf_op | source)
XLA Modules:
  0.0 73.2 jit_solution(15835368961031968128)
XLA Ops:
  0.6 70.7 %shard_map.49 = (f32[32,2048]{1,0:T(8,128)S(1)}, f32[16,128]{1,0:T(8,128)S(1)}, f32[8,128]{1,0:T(8,128)S(1)}) custom-call(bf16[32,2048]{1,0:T(8,128)(2,1)} %bitcast.7, bf16[1024,256]{1,0:T(8,128)(2,1)} %cb_hbm.1), custom_call_target="tpu_custom_call" | custom-call | tf_op jit(solution)/shard_map/pallas_call | solution.py:405
  71.3 0.7 copy.8
  72.1 0.6 copy.9
  72.7 0.6 copy.10

commit v4 on v3

--- a/solution.py
+++ b/solution.py
@@ -19,6 +19,7 @@
 CHUNK = 256
 TILE = 256
 PARTS = 4
+LEVELS = 7.0
 VMEM_BYTES = 48 * 1024 * 1024
 SIDE = 4
 MESH = pl.DeviceIdType.MESH
@@ -48,7 +49,7 @@
     cb, cbf, R, K, K2, inv_row, inv_col, tacc, W, tsend, cinv, wbuf, colbuf, rowbuf, sbuf,
     rows2, a2, r2, mix, shares_a, shares_b, softT, land,
     in_sem, ring_send, ring_recv, col_send, col_recv, row_send, row_recv,
-    z_send, z_recv, plane_send, plane_recv, pair_send, pair_recv, out_send, out_recv,
+    w_send, w_recv, z_send, z_recv, plane_send, plane_recv, pair_send, pair_recv, out_send, out_recv,
 ):
     me_i = lax.axis_index("items")
     me_z = lax.axis_index("codes")
@@ -213,13 +214,22 @@
     groups = codes // 8
     lane_chunks = rows // LANES
 
-    def exchange(buf, mine_at, count, axis, send_sem, recv_sem):
-        def send(k, carry):
-            ref = buf.at[mine_at]
-            remote(ref, ref, send_sem, recv_sem, {axis: lax.rem(mine_at + k, count)}).start()
-            return carry
-
-        lax.fori_loop(1, count, send, 0)
+    ring_order = sorted(range(1, codes_n), key=lambda k: -min(k, codes_n - k))
+    plane_order = sorted(
+        [(dx, dy, dc) for dx in range(SIDE) for dy in range(SIDE) for dc in range(2)],
+        key=lambda o: -(min(o[0], SIDE - o[0]) + min(o[1], SIDE - o[1])),
+    )
+
+    def exchange_codes(ref, send_sem, recv_sem):
+        for k in ring_order:
+            to = {"codes": lax.rem(me_z + k, codes_n)}
+            remote(ref, ref, send_sem, recv_sem, to).start()
+
+    def exchange_items(ref, send_sem, recv_sem):
+        for dx, dy, dc in plane_order:
+            if dx or dy or dc:
+                to = at_plane(lax.rem(x + dx, SIDE), lax.rem(y + dy, SIDE), lax.rem(core + dc, 2))
+                remote(ref, ref, send_sem, recv_sem, to).start()
 
     def all_but_one(buf, count, sem):
         wait_bytes(buf.at[pl.ds(0, count - 1)], sem)
@@ -273,7 +283,7 @@
             blockT = jnp.transpose(tacc[b * LANES:(b + 1) * LANES, :])
             tsend[b:b + 1, :] = jnp.sum(blockT, axis=0, keepdims=True)
         colbuf[it, me_i] = tsend[...]
-        exchange(colbuf.at[it], me_i, items_n, "items", col_send.at[it], col_recv.at[it])
+        exchange_items(colbuf.at[it, me_i], col_send.at[it], col_recv.at[it])
         if it == 0:
             for d, h, u, then in plan:
                 hop(d, h, u).wait_send()
@@ -303,14 +313,15 @@
         if last:
             w_ref[...] = w * math.exp(SHIFT)
             wbuf[me_z] = w * (1.0 / total_codes)
-            exchange(wbuf, me_z, codes_n, "codes", row_send.at[it], row_recv.at[it])
+            for k in ring_order:
+                remote(wbuf.at[me_z], wbuf.at[me_z], w_send, w_recv.at[k],
+                       {"codes": lax.rem(me_z + k, codes_n)}).start()
             for past in (1, 2):
                 all_but_one(colbuf.at[past], items_n, col_send.at[past])
             all_but_one(rowbuf.at[1], codes_n, row_send.at[1])
             for part in range(PARTS):
                 plane_wait(1 + part, plane_send)
                 pair_copy(part).wait_send()
-            all_but_one(wbuf, codes_n, row_recv.at[it])
             break
         for b in range(codes // LANES):
             W[b * LANES:(b + 1) * LANES, :] = jnp.transpose(
@@ -331,7 +342,7 @@
         for q in range(lane_chunks):
             s_ref[q:q + 1, :] = jnp.sum(acc[q], axis=0, keepdims=True)
         rowbuf[it, me_z] = s_ref[...]
-        exchange(rowbuf.at[it], me_z, codes_n, "codes", row_send.at[it], row_recv.at[it])
+        exchange_codes(rowbuf.at[it, me_z], row_send.at[it], row_recv.at[it])
         if it == 1:
             for part in (0, 1):
                 pair_copy(part).wait_recv()
@@ -342,52 +353,71 @@
     def part_of(z):
         return pl.ds(pl.multiple_of(z * feats, feats), feats)
 
-    def shares_of(z, at, out):
+    def shares_of(z, at, first, out):
         total = []
         for q in range(codes // LANES):
-            value = K2[at, z * codes + q * LANES:z * codes + (q + 1) * LANES] * wbuf[z, q:q + 1, :]
+            lanes = slice(z * codes + q * LANES, z * codes + (q + 1) * LANES)
+            value = K2[at, lanes] * wbuf[z, q:q + 1, :]
             total.append(value)
             out[:, q * LANES:(q + 1) * LANES] = value.astype(jnp.bfloat16)
-        r2[...] = tree_sum(total) if z == 0 else r2[...] + tree_sum(total)
-
-    def mix_of(z, src):
+        r2[...] = tree_sum(total) if first else r2[...] + tree_sum(total)
+
+    def mix_of(z, first, src):
         some = jnp.dot(src[...], cbf[z].reshape(codes, F), preferred_element_type=jnp.float32)
-        mix[...] = some if z == 0 else mix[...] + some
-
+        mix[...] = some if first else mix[...] + some
+
+    def encode(b, values):
+        near = values.astype(jnp.bfloat16)
+        wide = near.astype(jnp.float32)
+        left = (values - wide) * (LEVELS * 256.0 / jnp.maximum(jnp.abs(wide), 1e-30))
+        left = jnp.clip(jnp.round(left), -LEVELS, LEVELS).reshape(codes_n, 2, feats // 2, LANES)
+        softT[b, :, :feats, :] = near.reshape(codes_n, feats, LANES)
+        softT[b, :, feats:, :] = (left[:, 0] * 16.0 + left[:, 1]).astype(jnp.bfloat16)
+
+    def decode(coded):
+        wide = coded[:feats, :].astype(jnp.float32)
+        both = coded[feats:, :].astype(jnp.float32)
+        high = jnp.round(both * (1.0 / 16.0))
+        left = jnp.concatenate([high, both - 16.0 * high], axis=0)
+        return wide + jnp.abs(wide) * (left * (1.0 / (LEVELS * 256.0)))
+
+    for k in ring_order:
+        wait_bytes(wbuf.at[0], w_recv.at[k])
     buffers = (shares_a, shares_b)
-    for b in range(mine // LANES):
-        at = slice(b * LANES, (b + 1) * LANES)
-        shares_of(0, at, buffers[0])
+
+    def half_step(b, carry):
+        at = pl.ds(pl.multiple_of(b * LANES, LANES), LANES)
         for z in range(codes_n):
-            if z + 1 < codes_n:
-                shares_of(z + 1, at, buffers[(z + 1) % 2])
-            mix_of(z, buffers[z % 2])
+            shares_of(z, at, z == 0, buffers[z % 2])
+            if z > 0:
+                mix_of(z - 1, z == 1, buffers[(z - 1) % 2])
+        mix_of(codes_n - 1, False, buffers[(codes_n - 1) % 2])
         scale = 1.0 / jnp.sum(jnp.transpose(r2[...]), axis=0, keepdims=True)
-        sbuf[me_z, b:b + 1, :] = scale
-        softT[b] = jnp.transpose(mix[...]) * scale
-        my_lanes = pl.ds(pl.multiple_of(me_z * mine + b * LANES, LANES), LANES)
-
-        def send_out(k, carry, b=b, my_lanes=my_lanes):
+        sbuf[me_z, pl.ds(b, 1), :] = scale
+        encode(b, jnp.transpose(mix[...]) * scale)
+        for k in ring_order:
             z = lax.rem(me_z + k, codes_n)
-            remote(softT.at[b, part_of(z), :], land.at[:, my_lanes],
-                   out_send.at[b], out_recv.at[b], {"codes": z}).start()
-            return carry
-
-        lax.fori_loop(1, codes_n, send_out, 0)
-        land[:, my_lanes] = softT[b, part_of(me_z), :]
-    exchange(sbuf, me_z, codes_n, "codes", out_send.at[2], out_recv.at[2])
-    all_but_one(wbuf, codes_n, row_send.at[ITERS - 1])
-
-    for b in range(mine // LANES):
-        wait_bytes(land.at[:, pl.ds(0, (codes_n - 1) * LANES)], out_recv.at[b])
+            remote(softT.at[b, z], land.at[b, me_z], out_send.at[b], out_recv.at[b],
+                   {"codes": z}).start()
+        land[b, me_z] = softT[b, me_z]
+        return carry
+
+    lax.fori_loop(0, mine // LANES, half_step, 0)
+    exchange_codes(sbuf.at[me_z], out_send.at[2], out_recv.at[2])
+    all_but_one(wbuf, codes_n, w_send)
+
     all_but_one(sbuf, codes_n, out_recv.at[2])
-    soft_ref[...] = land[...]
     for z in range(codes_n):
         for b in range(mine // LANES):
             n = z * (mine // LANES) + b
             s_ref[n:n + 1, :] = sbuf[z, b:b + 1, :]
     for b in range(mine // LANES):
-        wait_bytes(land.at[:, pl.ds(0, (codes_n - 1) * LANES)], out_send.at[b])
+        all_but_one(land.at[b], codes_n, out_recv.at[b])
+        for z in range(codes_n):
+            n = z * (mine // LANES) + b
+            soft_ref[:, n * LANES:(n + 1) * LANES] = decode(land[b, z])
+    for b in range(mine // LANES):
+        all_but_one(land.at[b], codes_n, out_send.at[b])
     all_but_one(sbuf, codes_n, out_send.at[2])
 
 
@@ -435,12 +465,13 @@
             pltpu.VMEM((LANES, F), f32),
             pltpu.VMEM((LANES, codes), bf16),
             pltpu.VMEM((LANES, codes), bf16),
-            pltpu.VMEM((mine // LANES, F, LANES), f32),
-            pltpu.VMEM((feats, rows), f32),
+            pltpu.VMEM((mine // LANES, codes_n, feats + feats // 2, LANES), bf16),
+            pltpu.VMEM((mine // LANES, codes_n, feats + feats // 2, LANES), bf16),
             dma((chunks + 3,)),
             dma((2, half, chunks + 1)),
             dma((2, half, chunks + 1)),
-            dma((ITERS,)), dma((ITERS,)), dma((ITERS,)), dma((ITERS,)),
+            dma((ITERS,)), dma((ITERS,)), dma((ITERS - 1,)), dma((ITERS - 1,)),
+            dma, dma((codes_n,)),
             dma, dma,
             dma((PARTS + 1, 2)), dma((PARTS + 1, 2)),
             dma((PARTS,)), dma((PARTS,)),

time: 74.6 us -> 72 us (0.965)
  Pallas kernels: 70.7 us -> 68.3 us
    pallas_call x1, Pallas kernels: 70.7 us -> 68.3 us  [shards(): pl.pallas_call(functools.partial(kernel, items_n, codes_n, float(rows * i...]
where the time goes in v4:
time: 72 us; the launch traced here: 70.9 us
  Pallas kernels  68.3 us (95%)
  local copies, waits for them, and re-layouts  1.9 us (3%)
    pallas_call x1, Pallas kernels, shards(): pl.pallas_call(functools.partial(kernel, items_n, codes_n, float(rows * i...  68.3 us
    unnamed x3, local copies, waits for them, and re-layouts  1.9 us

profile of v4, /device:TPU:2, one launch (start us, length us, event | category | flops | bytes accessed | tf_op | source)
XLA Modules:
  0.0 70.9 jit_solution(13429726780103220272)
XLA Ops:
  0.6 68.3 %shard_map.49 = (f32[32,2048]{1,0:T(8,128)S(1)}, f32[16,128]{1,0:T(8,128)S(1)}, f32[8,128]{1,0:T(8,128)S(1)}) custom-call(bf16[32,2048]{1,0:T(8,128)(2,1)} %bitcast.7, bf16[1024,256]{1,0:T(8,128)(2,1)} %cb_hbm.1), custom_call_target="tpu_custom_call" | custom-call | tf_op jit(solution)/shard_map/pallas_call | solution.py:435
  69.0 0.7 copy.8
  69.7 0.6 copy.9
  70.3 0.6 copy.10

commit v5 on v4

--- a/solution.py
+++ b/solution.py
@@ -45,8 +45,8 @@
 
 def kernel(
     items_n, codes_n, total_items, total_codes,
-    rt_hbm, cb_hbm, soft_ref, s_ref, w_ref,
-    cb, cbf, R, K, K2, inv_row, inv_col, tacc, W, tsend, cinv, wbuf, colbuf, rowbuf, sbuf,
+    rt_hbm, cb_hbm, out_ref,
+    s_ref, cb, cbf, R, K, K2, inv_row, inv_col, tacc, W, tsend, cinv, wbuf, colbuf, rowbuf, sbuf,
     rows2, a2, r2, mix, shares_a, shares_b, softT, land,
     in_sem, ring_send, ring_recv, col_send, col_recv, row_send, row_recv,
     w_send, w_recv, z_send, z_recv, plane_send, plane_recv, pair_send, pair_recv, out_send, out_recv,
@@ -311,7 +311,9 @@
             plane_start(2 + 2 * it)
         w = total_items / jnp.sum(colbuf[it], axis=0)
         if last:
-            w_ref[...] = w * math.exp(SHIFT)
+            w_out = w * math.exp(SHIFT)
+            for b in range(codes // LANES):
+                out_ref[feats + 1:feats + 2, b * LANES:(b + 1) * LANES] = w_out[b:b + 1, :]
             wbuf[me_z] = w * (1.0 / total_codes)
             for k in ring_order:
                 remote(wbuf.at[me_z], wbuf.at[me_z], w_send, w_recv.at[k],
@@ -394,7 +396,7 @@
         mix_of(codes_n - 1, False, buffers[(codes_n - 1) % 2])
         scale = 1.0 / jnp.sum(jnp.transpose(r2[...]), axis=0, keepdims=True)
         sbuf[me_z, pl.ds(b, 1), :] = scale
-        encode(b, jnp.transpose(mix[...]) * scale)
+        encode(b, jnp.transpose(mix[...]))
         for k in ring_order:
             z = lax.rem(me_z + k, codes_n)
             remote(softT.at[b, z], land.at[b, me_z], out_send.at[b], out_recv.at[b],
@@ -410,12 +412,12 @@
     for z in range(codes_n):
         for b in range(mine // LANES):
             n = z * (mine // LANES) + b
-            s_ref[n:n + 1, :] = sbuf[z, b:b + 1, :]
+            out_ref[feats:feats + 1, n * LANES:(n + 1) * LANES] = sbuf[z, b:b + 1, :]
     for b in range(mine // LANES):
         all_but_one(land.at[b], codes_n, out_recv.at[b])
         for z in range(codes_n):
             n = z * (mine // LANES) + b
-            soft_ref[:, n * LANES:(n + 1) * LANES] = decode(land[b, z])
+            out_ref[:feats, n * LANES:(n + 1) * LANES] = decode(land[b, z])
     for b in range(mine // LANES):
         all_but_one(land.at[b], codes_n, out_send.at[b])
     all_but_one(sbuf, codes_n, out_send.at[2])
@@ -432,18 +434,15 @@
     hbm = pl.BlockSpec(memory_space=pltpu.HBM)
     vmem = pl.BlockSpec(memory_space=pltpu.VMEM)
     dma = pltpu.SemaphoreType.DMA
-    softT, items_scale, code_weights = pl.pallas_call(
+    out = pl.pallas_call(
         functools.partial(
             kernel, items_n, codes_n, float(rows * items_n), float(codes * codes_n)
         ),
-        out_shape=(
-            jax.ShapeDtypeStruct((feats, rows), f32),
-            jax.ShapeDtypeStruct((rows // LANES, LANES), f32),
-            jax.ShapeDtypeStruct((codes // LANES, LANES), f32),
-        ),
+        out_shape=jax.ShapeDtypeStruct((feats + 8, rows), f32),
         in_specs=[hbm, hbm],
-        out_specs=(vmem, vmem, vmem),
+        out_specs=vmem,
         scratch_shapes=[
+            pltpu.VMEM((rows // LANES, LANES), f32),
             pltpu.VMEM((codes, F), bf16),
             pltpu.VMEM((codes_n, SIDE, SIDE, 2, 2, 16, F), bf16),
             pltpu.VMEM((chunks, F, CHUNK), bf16),
@@ -481,7 +480,8 @@
             collective_id=0, has_side_effects=True, vmem_limit_bytes=VMEM_BYTES
         ),
     )(pltpu.with_memory_space_constraint(residuals.T, pltpu.HBM), pltpu.with_memory_space_constraint(codebook, pltpu.HBM))
-    return softT.T, items_scale.reshape(rows), code_weights.reshape(codes)
+    items_scale = out[feats]
+    return (out[:feats] * items_scale[None, :]).T, items_scale, out[feats + 1, :codes]
 
 
 def solution(mesh):

time: 72 us -> 71.6 us (level)
  local copies, waits for them, and re-layouts: 1.9 us -> 0.61 us
  other arithmetic: 0 us -> 0.73 us
    unnamed x3 -> x2, local copies, waits for them, and re-layouts: 1.9 us -> 0.01 us
    transpose x0 -> x1, other arithmetic: none -> 0.73 us  [shards(): return ((out[:feats] * items_scale[None, :]).T, items_scale, out[feats +...]
where the time goes in v5:
time: 71.6 us; the launch traced here: 70.5 us
  Pallas kernels  68.5 us (96%)
  other arithmetic  0.73 us (1%)
    pallas_call x1, Pallas kernels, shards(): pl.pallas_call(functools.partial(kernel, items_n, codes_n, float(rows * i...  68.5 us

profile of v5, /device:TPU:2, one launch (start us, length us, event | category | flops | bytes accessed | tf_op | source)
XLA Modules:
  0.0 70.5 jit_solution(14067928554503384648)
XLA Ops:
  0.6 68.5 %shard_map.49 = f32[40,2048]{1,0:T(8,128)S(1)} custom-call(bf16[32,2048]{1,0:T(8,128)(2,1)} %bitcast.5, bf16[1024,256]{1,0:T(8,128)(2,1)} %cb_hbm.1), custom_call_target="tpu_custom_call" | custom-call | tf_op jit(solution)/shard_map/pallas_call | solution.py:437
  69.2 0.6 slice.11
  69.8 0.0 copy-start
  69.8 0.7 %multiply_bitcast_fusion = f32[2048,32]{0,1:T(8,128)} fusion(f32[40,2048]{1,0:T(8,128)S(1)} %shard_map.49, f32[2048]{0:T(1024)S(1)} %bitcast.6), kind=kLoop, calls=%fused_computation | loop fusion | flops 65536 | bytes 532480 | tf_op jit(solution)/shard_map/transpose | solution.py:484
  70.5 0.0 copy-done
  (1 shorter events, 0.0 us)
Async XLA Ops:
  69.8 0.7 %copy-start = (f32[1,2048]{1,0:T(1,128)}, f32[1,2048]{1,0:T(1,128)S(1)}, u32[]{:S(2)}) copy-start(f32[1,2048]{1,0:T(1,128)S(1)} %slice.10) | copy-start | bytes 24580

commit v6 on v4

--- a/solution.py
+++ b/solution.py
@@ -295,7 +295,8 @@
                 pair_copy(part).start()
             plane_wait(0, plane_send)
             all_but_one(colbuf.at[0], items_n, col_send.at[0])
-            all_but_one(rowbuf.at[0], codes_n, row_send.at[0])
+            for side in range(2):
+                all_but_one(rowbuf.at[0, side], codes_n, row_send.at[0, side])
             all_but_one(cinv, codes_n, z_recv)
             all_but_one(cinv, codes_n, z_send)
         if last:
@@ -318,7 +319,8 @@
                        {"codes": lax.rem(me_z + k, codes_n)}).start()
             for past in (1, 2):
                 all_but_one(colbuf.at[past], items_n, col_send.at[past])
-            all_but_one(rowbuf.at[1], codes_n, row_send.at[1])
+            for side in range(2):
+                all_but_one(rowbuf.at[1, side], codes_n, row_send.at[1, side])
             for part in range(PARTS):
                 plane_wait(1 + part, plane_send)
                 pair_copy(part).wait_send()
@@ -328,27 +330,33 @@
                 jnp.broadcast_to(w[b:b + 1, :], (LANES, LANES))
             )
 
-        def row_step(g, acc):
-            at = pl.ds(pl.multiple_of(g * 8, 8), 8)
-            weight = W[at, :]
-            return tuple(
-                acc[q] + K[at, q * LANES:(q + 1) * LANES] * weight for q in range(lane_chunks)
+        width = lane_chunks // 2
+        for side in range(2):
+            def row_step(g, acc, side=side):
+                at = pl.ds(pl.multiple_of(g * 8, 8), 8)
+                weight = W[at, :]
+                return tuple(
+                    acc[q] + K[at, (side * width + q) * LANES:(side * width + q + 1) * LANES] * weight
+                    for q in range(width)
+                )
+
+            acc = lax.fori_loop(
+                0, groups, row_step,
+                tuple(jnp.zeros((8, LANES), jnp.float32) for _ in range(width)), unroll=8,
             )
-
-        acc = lax.fori_loop(
-            0, groups, row_step,
-            tuple(jnp.zeros((8, LANES), jnp.float32) for _ in range(lane_chunks)), unroll=4,
-        )
-        for q in range(lane_chunks):
-            s_ref[q:q + 1, :] = jnp.sum(acc[q], axis=0, keepdims=True)
-        rowbuf[it, me_z] = s_ref[...]
-        exchange_codes(rowbuf.at[it, me_z], row_send.at[it], row_recv.at[it])
+            for q in range(width):
+                rowbuf[it, side, me_z, q:q + 1, :] = jnp.sum(acc[q], axis=0, keepdims=True)
+            exchange_codes(
+                rowbuf.at[it, side, me_z], row_send.at[it, side], row_recv.at[it, side]
+            )
         if it == 1:
             for part in (0, 1):
                 pair_copy(part).wait_recv()
                 second_tile(part)
-        all_but_one(rowbuf.at[it], codes_n, row_recv.at[it])
-        s_ref[...] = total_codes / jnp.sum(rowbuf[it], axis=0)
+        for side in range(2):
+            all_but_one(rowbuf.at[it, side], codes_n, row_recv.at[it, side])
+            at = slice(side * width, (side + 1) * width)
+            s_ref[at, :] = total_codes / jnp.sum(rowbuf[it, side], axis=0)
 
     def part_of(z):
         return pl.ds(pl.multiple_of(z * feats, feats), feats)
@@ -457,7 +465,7 @@
             pltpu.VMEM((codes_n, codes // LANES, LANES), f32),
             pltpu.VMEM((codes_n, codes // LANES, LANES), f32),
             pltpu.VMEM((ITERS, items_n, codes // LANES, LANES), f32),
-            pltpu.VMEM((ITERS - 1, codes_n, rows // LANES, LANES), f32),
+            pltpu.VMEM((ITERS - 1, 2, codes_n, rows // LANES // 2, LANES), f32),
             pltpu.VMEM((codes_n, mine // LANES, LANES), f32),
             pltpu.VMEM((mine, F), bf16),
             pltpu.VMEM((mine, LANES), f32),
@@ -470,7 +478,7 @@
             dma((chunks + 3,)),
             dma((2, half, chunks + 1)),
             dma((2, half, chunks + 1)),
-            dma((ITERS,)), dma((ITERS,)), dma((ITERS - 1,)), dma((ITERS - 1,)),
+            dma((ITERS,)), dma((ITERS,)), dma((ITERS - 1, 2)), dma((ITERS - 1, 2)),
             dma, dma((codes_n,)),
             dma, dma,
             dma((PARTS + 1, 2)), dma((PARTS + 1, 2)),

time: 72 us -> 71.9 us (level)
  no operation moved by 1% of the time
where the time goes in v6:
time: 71.9 us; the launch traced here: 70.8 us
  Pallas kernels  68.3 us (95%)
  local copies, waits for them, and re-layouts  1.9 us (3%)
    pallas_call x1, Pallas kernels, shards(): pl.pallas_call(functools.partial(kernel, items_n, codes_n, float(rows * i...  68.3 us
    unnamed x3, local copies, waits for them, and re-layouts  1.9 us

profile of v6, /device:TPU:2, one launch (start us, length us, event | category | flops | bytes accessed | tf_op | source)
XLA Modules:
  0.0 70.8 jit_solution(7726314188206062370)
XLA Ops:
  0.6 68.3 %shard_map.49 = (f32[32,2048]{1,0:T(8,128)S(1)}, f32[16,128]{1,0:T(8,128)S(1)}, f32[8,128]{1,0:T(8,128)S(1)}) custom-call(bf16[32,2048]{1,0:T(8,128)(2,1)} %bitcast.7, bf16[1024,256]{1,0:T(8,128)(2,1)} %cb_hbm.1), custom_call_target="tpu_custom_call" | custom-call | tf_op jit(solution)/shard_map/pallas_call | solution.py:443
  68.9 0.7 copy.8
  69.6 0.6 copy.9
  70.2 0.6 copy.10
